TPU v7x, 32 devices: a whole 2x2x4 slice. The times are simulated.
32 devices in a mesh: mode: 8 (over z, y), slab: 4 (over x, core).
Axes of the slice: x: 2, y: 2, z: 4, core: 2. Of those that a mesh axis runs over, the one named last changes fastest.
Arguments:
- adjoint: float32 [32, 2, 5, 65536], P('mode', None, None, 'slab'), may hold values from -6 to 6
- source: float32 [32, 2, 5, 65536], P('mode', None, None, 'slab'), may hold values from -6 to 6
- derivative: float32 [64, 64], replicated, may hold values from -0.75 to 0.75
- lift_matrix: float32 [64, 64], replicated, may hold values from -0.75 to 0.75
- jacobian: float32 [5, 5], replicated, may hold values from -2.5 to 2.5
- harmonics: float32 [5, 65536], P(None, 'slab'), may hold values from -6 to 6
- swirl_rate: float32 [65536], P('slab'), may hold values from -6 to 6
- coupling: float32 [32, 5, 2, 4], P('mode'), may hold values from -1 to 1
- mode_number: int32 [32], P('mode'), may hold values from -16 to 16, as said below
- partner: int32 [32], P('mode'), may hold values from 0 to 31, as said below
- upstream: int32 [1024], P('slab'), may hold values from 0 to 270, as said below
- face_list: int32 [64], P('slab'), may hold values from 0 to 255, as said below
Outputs:
- residual: float32 [32, 2, 5, 65536], P('mode', None, None, 'slab')
- sensitivity: float32 [32, 2, 5, 65536], P('mode', None, None, 'slab')
Inputs may be any that keep to these rules, and one draw needn't show every extreme that they name: `mode_number`: never 0; every number from 1 to 16 appears once with each sign. partner[partner[m]] = m, mode_number[partner[m]] = -mode_number[m], and partner[m] lies in group (m // 4 + 16 // 4) mod (8). `upstream`: for the element at position e of its slab: below 16, the value is e, naming face e of the previous slab; otherwise the value minus 16 is a local element of the same slab before e. `face_list`: each block of 16 entries holds distinct local element numbers of its slab.
All inputs are finite; a program needn't handle non-finite values.
Results may differ from a plain program's by a relative error of at most 0.0001.
Values sent between devices are 32-bit elements; how exact they have to be, the bound alone decides.
A program may use at most 128 MiB of HBM per device.

v0:
```python
import jax
import jax.numpy as jnp
from jax import lax
from jax.sharding import PartitionSpec as P

TAPS = 5


def shifted(block, axis, distance):
    devices = range(lax.axis_size(axis))
    route = [((i - distance) % len(devices), i) for i in devices]
    return lax.ppermute(block, axis, route)


def shifted_2(block, axis, distance):
    devices = range(lax.axis_size(axis))
    route = [(i - distance, i) for i in devices if i - distance in devices]
    return lax.ppermute(block, axis, route)


def from_partner(block, axis, bit):
    count = lax.axis_size(axis)
    route = []
    for low in range(count):
        high = low | 1 << bit
        if high != low and high < count:
            route += [(low, high), (high, low)]
    return lax.ppermute(block, axis, route)


def per_device(
    adjoint,
    source,
    derivative,
    lift_matrix,
    jacobian,
    harmonics,
    swirl_rate,
    coupling,
    mode_number,
    partner,
    upstream,
    face_list,
):
    highest = lax.Precision.HIGHEST
    modes_here = adjoint.shape[0]
    variables = adjoint.shape[2]
    cells_here = adjoint.shape[3]
    nodes = derivative.shape[0]
    elements = cells_here // nodes
    face_count = face_list.shape[0]
    center = TAPS // 2
    highest_mode = modes_here * lax.axis_size("mode") // 2

    def couple_tap(panel, tap):
        real_w = coupling[:, tap, 0]
        imag_w = coupling[:, tap, 1]
        real_part = jnp.einsum("ab,bvx->avx", real_w, panel[:, 0], precision=highest) - jnp.einsum(
            "ab,bvx->avx", imag_w, panel[:, 1], precision=highest
        )
        imag_part = jnp.einsum("ab,bvx->avx", real_w, panel[:, 1], precision=highest) + jnp.einsum(
            "ab,bvx->avx", imag_w, panel[:, 0], precision=highest
        )
        return jnp.stack([real_part, imag_part], axis=1) * harmonics[tap][None, None, None, :]

    field = adjoint.reshape(modes_here, 2, variables, elements, nodes)
    faces_out = jnp.take(field, face_list, axis=3).reshape(
        modes_here, 2, variables, face_count * nodes
    )
    mixing = couple_tap(adjoint, center)
    upward = adjoint
    downward = adjoint
    for distance in range(1, center + 1):
        upward = shifted(upward, "mode", 1)
        downward = shifted(downward, "mode", -1)
        mixing = (
            mixing + couple_tap(upward, center + distance) + couple_tap(downward, center - distance)
        )
    halo = shifted_2(faces_out, "slab", 1).reshape(modes_here, 2, variables, face_count, nodes)
    extended = jnp.concatenate([halo, field], axis=3)
    upper = jnp.take(extended, upstream, axis=3)
    eye_two = jnp.eye(2, dtype=jnp.float32)
    derivative_pair = jnp.kron(eye_two, derivative.T)
    lift_pair = jnp.kron(eye_two, lift_matrix.T)
    paired_field = field.reshape(modes_here, 2, variables, elements // 2, 2 * nodes)
    paired_upper = upper.reshape(modes_here, 2, variables, elements // 2, 2 * nodes)
    meridional = jnp.dot(paired_field, derivative_pair, precision=highest) + jnp.dot(
        paired_upper, lift_pair, precision=highest
    )
    meridional = meridional.reshape(modes_here, 2, variables, cells_here)
    convective = jnp.einsum("wv,mcvx->mcwx", jacobian, meridional, precision=highest)
    factor = (mode_number.astype(jnp.float32) / highest_mode)[:, None, None] * swirl_rate[
        None, None, :
    ]
    azimuthal = jnp.stack([-factor * adjoint[:, 1], factor * adjoint[:, 0]], axis=1)
    residual = source - convective - azimuthal - mixing
    top_bit = lax.axis_size("mode").bit_length() - 2
    opposite_group = from_partner(residual, "mode", top_bit)
    opposite = jnp.take(opposite_group, partner % modes_here, axis=0)
    sensitivity = residual + jnp.stack([opposite[:, 0], -opposite[:, 1]], axis=1)
    return (residual, sensitivity)


def solution(mesh):
    in_specs = (
        P("mode", None, None, "slab"),
        P("mode", None, None, "slab"),
        P(),
        P(),
        P(),
        P(None, "slab"),
        P("slab"),
        P("mode", None, None, None),
        P("mode"),
        P("mode"),
        P("slab"),
        P("slab"),
    )
    out_specs = (P("mode", None, None, "slab"), P("mode", None, None, "slab"))
    return jax.shard_map(
        per_device, mesh=mesh, in_specs=in_specs, out_specs=out_specs, check_vma=False
    )
```

profile of v0, /device:TPU:0, one launch (start us, length us, event | category | flops | bytes accessed | tf_op | source)
XLA Modules:
  0.0 423.9 jit_solution(16463503322253538103)
XLA Ops:
  0.7 5.1 %copy.202 = f32[4,2,5,16384]{3,0,2,1:T(4,128)} copy(f32[4,2,5,16384]{3,1,2,0:T(2,128)} %param.12) | data formatting | bytes 5242880 | tf_op args[0]
  5.7 6.0 %collective-permute-start.2 = (f32[4,2,5,16384]{3,0,2,1:T(4,128)}, f32[4,2,5,16384]{3,0,2,1:T(4,128)}, u32[]{:S(2)}, u32[]{:S(2)}) collective-permute-start(f32[4,2,5,16384]{3,0,2,1:T(4,128)} %copy.202), channel_id=1, source_target_pairs={{4,0},{8,4},{12,8},{16,12},{20,16},{24,20},{28,24},{0,28},{5,1},{9... | collective-permute-start | bytes 7864328 | tf_op jit(solution)/shard_map/ppermute | solution.py:12
  11.8 4.5 %reshape.160 = f32[4,2,5,256,64]{4,3,1,2,0:T(8,128)} reshape(f32[4,2,5,16384]{3,1,2,0:T(2,128)S(1)} %copy-done.3) | data formatting | bytes 5242880 | tf_op jit(solution)/shard_map/reshape | solution.py:66
  16.5 8.2 %copy.182 = f32[4,2,5,256,64]{4,0,3,2,1:T(4,128)} copy(f32[4,2,5,256,64]{4,3,1,2,0:T(8,128)} %reshape.160) | data formatting | bytes 5242880 | tf_op jit(solution)/shard_map/reshape | solution.py:66
  34.0 3.8 copy_bitcast_fusion
  61.9 6.3 %pad_maximum_fusion = f32[4,2,5,272,64]{4,0,3,2,1:T(4,128)} fusion(f32[4,2,5,256,64]{4,0,3,2,1:T(4,128)} %copy.182, f32[4,2,5,16,64]{4,0,3,2,1:T(4,128)S(1)} %copy.184), kind=kLoop, calls=%fused_computation.7 | loop fusion | flops 696320 | bytes 5570560 | tf_op jit(solution)/shard_map/concatenate | solution.py:80
  68.2 9.2 %gather_fusion.1 = f32[256,4,2,5,64]{4,1,3,2,0:T(4,128)} fusion(f32[4,2,5,272,64]{4,0,3,2,1:T(4,128)} %pad_maximum_fusion, s32[1024]{0:T(1024)S(1)} %pad_clamp_fusion.1), kind=kCustom, calls=%fused_computation.1 | custom fusion | bytes 5243904 | tf_op jit(solution)/shard_map/jit(_take)/gather | solution.py:81
  77.4 4.4 %select_bitcast_fusion = f32[4,2,5,256,64]{4,0,2,1,3:T(4,128)S(1)} fusion(f32[256,4,2,5,64]{4,1,3,2,0:T(4,128)} %gather_fusion.1, pred[256,64]{1,0:T(8,128)(4,1)S(1)} %broadcast_in_dim.56), kind=kLoop, calls=%fused_computation.8 | loop fusion | flops 655360 | bytes 5259264 | tf_op jit(solution)/shard_map/jit(_take)/select_n | solution.py:81
  85.0 4.0 select_n.49
  96.4 4.3 %reshape.205 = f32[4,2,5,16384]{3,2,1,0:T(8,128)} reshape(f32[4,2,5,128,128]{4,3,2,1,0:T(8,128)} %copy.232) | data formatting | bytes 5242880 | tf_op jit(solution)/shard_map/reshape | solution.py:90
  100.7 21.4 %collective-permute-done.2 = f32[4,2,5,16384]{3,0,2,1:T(4,128)} collective-permute-done((f32[4,2,5,16384]{3,0,2,1:T(4,128)}, f32[4,2,5,16384]{3,0,2,1:T(4,128)}, u32[]{:S(2)}, u32[]{:S(2)}) %collective-permute-start.2) | collective-permute-done | bytes 2621472 | tf_op jit(solution)/shard_map/ppermute | solution.py:12
  125.6 3.6 fusion.26
  129.2 3.6 fusion.25
  132.7 3.6 fusion.28
  139.3 4.9 %fusion.13 = (f32[4,1,5,16384]{3,2,1,0:T(8,128)}, f32[4,1,5,16384]{3,2,1,0:T(8,128)}) fusion(f32[4,5,16384]{2,0,1:T(4,128)S(1)} %fusion.25, f32[4,5,16384]{2,0,1:T(4,128)S(1)} %fusion.27, f32[4,5,16384]{2,0,1:T(4,128)S(1)} %fusion.28, f32[4,5,16384]{2,0,1:T(4,128)S(1)} %fusion.26), kind=kLoop, calls=%fused_computation.37 | loop fusion | flops 655360 | bytes 7864320 | tf_op jit(solution)/shard_map/stack | solution.py:64
  151.4 3.6 fusion.21
  154.9 4.0 fusion.24
  159.0 5.0 %fusion.15 = (f32[4,1,5,16384]{3,2,1,0:T(8,128)}, f32[4,1,5,16384]{3,2,1,0:T(8,128)}) fusion(f32[4,5,16384]{2,0,1:T(4,128)S(1)} %fusion.21, f32[4,5,16384]{2,0,1:T(4,128)S(1)} %fusion.23, f32[4,5,16384]{2,0,1:T(4,128)S(1)} %fusion.24, f32[4,5,16384]{2,0,1:T(4,128)S(1)} %fusion.22), kind=kLoop, calls=%fused_computation.41 | loop fusion | flops 655360 | bytes 7864320 | tf_op jit(solution)/shard_map/stack | solution.py:64
  164.0 87.0 %collective-permute-done.4 = f32[4,2,5,16384]{3,0,2,1:T(4,128)S(1)} collective-permute-done((f32[4,2,5,16384]{3,0,2,1:T(4,128)}, f32[4,2,5,16384]{3,0,2,1:T(4,128)S(1)}, u32[]{:S(2)}, u32[]{:S(2)}) %collective-permute-start.4) | collective-permute-done | bytes 2621472 | tf_op jit(solution)/shard_map/ppermute | solution.py:12
  260.4 5.0 %fusion.9 = (f32[4,1,5,16384]{3,2,1,0:T(8,128)}, f32[4,1,5,16384]{3,2,1,0:T(8,128)}) fusion(f32[4,5,16384]{2,0,1:T(4,128)S(1)} %fusion.33, f32[4,5,16384]{2,0,1:T(4,128)S(1)} %fusion.35, f32[4,5,16384]{2,0,1:T(4,128)S(1)} %fusion.36, f32[4,5,16384]{2,0,1:T(4,128)S(1)} %fusion.34), kind=kLoop, calls=%fused_computation.29 | loop fusion | flops 655360 | bytes 7864320 | tf_op jit(solution)/shard_map/stack | solution.py:64
  274.7 5.0 %fusion.11 = (f32[4,1,5,16384]{3,2,1,0:T(8,128)}, f32[4,1,5,16384]{3,2,1,0:T(8,128)}) fusion(f32[4,5,16384]{2,0,1:T(4,128)S(1)} %fusion.29, f32[4,5,16384]{2,0,1:T(4,128)S(1)} %fusion.31, f32[4,5,16384]{2,0,1:T(4,128)S(1)} %fusion.32, f32[4,5,16384]{2,0,1:T(4,128)S(1)} %fusion.30), kind=kLoop, calls=%fused_computation.33 | loop fusion | flops 655360 | bytes 7864320 | tf_op jit(solution)/shard_map/stack | solution.py:64
  279.7 11.1 %fusion.2 = f32[4,2,5,16384]{3,2,1,0:T(8,128)S(1)} fusion(f32[4,2,5,16384]{3,2,1,0:T(8,128)S(1)} %copy-done.4, f32[4,1,5,16384]{3,2,1,0:T(8,128)S(1)} %copy-done.8, f32[4,1,5,16384]{3,2,1,0:T(8,128)} %get-tuple-element.41, f32[4,1,5,16384]{3,2,1,0:T(8,128)S(1)} %copy-done.7, f32[4,1,5,16384]{3,2,1,0:T(8,128)S(1)} %copy-done.6, ...), kind=kOutput, calls=%fused_computation.6 | convolution fusion | flops 51118080 | bytes 23920740 | tf_op jit(solution)/shard_map/wv,mcvx->mcwx/dot_general | solution.py:91
  298.6 108.2 %collective-permute-done.5 = f32[4,2,5,16384]{3,0,2,1:T(4,128)S(1)} collective-permute-done((f32[4,2,5,16384]{3,0,2,1:T(4,128)S(1)}, f32[4,2,5,16384]{3,0,2,1:T(4,128)S(1)}, u32[]{:S(2)}, u32[]{:S(2)}) %collective-permute-start.5) | collective-permute-done | bytes 2621472 | tf_op jit(solution)/shard_map/ppermute | solution.py:28
  410.3 5.1 %gather_fusion.2 = f32[4,2,5,16384]{3,1,2,0:T(2,128)S(1)} fusion(f32[4,2,5,16384]{3,1,2,0:T(2,128)} %copy.221, s32[1024]{0:T(1024)S(1)} %pad_clamp_fusion), kind=kCustom, calls=%fused_computation.2 | custom fusion | bytes 5242896 | tf_op jit(solution)/shard_map/jit(_take)/gather | solution.py:99
  (103 shorter events, 95.9 us)
Async XLA Ops:
  0.6 279.1 %copy-start = (f32[5,5]{1,0:T(8,128)S(1)}, f32[5,5]{1,0:T(8,128)}, u32[]{:S(2)}) copy-start(f32[5,5]{1,0:T(8,128)} %param.16) | copy-start | bytes 304
  0.6 11.1 %copy-start.3 = (f32[4,2,5,16384]{3,1,2,0:T(2,128)S(1)}, f32[4,2,5,16384]{3,1,2,0:T(2,128)}, u32[]{:S(2)}) copy-start(f32[4,2,5,16384]{3,1,2,0:T(2,128)} %param.12) | copy-start | bytes 7864324
  0.7 11.1 %copy-start.15 = (s32[16]{0:T(128)S(1)}, s32[16]{0:T(128)}, u32[]{:S(2)}) copy-start(s32[16]{0:T(128)} %param.23) | copy-start | bytes 196
  5.7 116.3 %collective-permute-start.2 = (f32[4,2,5,16384]{3,0,2,1:T(4,128)}, f32[4,2,5,16384]{3,0,2,1:T(4,128)}, u32[]{:S(2)}, u32[]{:S(2)}) collective-permute-start(f32[4,2,5,16384]{3,0,2,1:T(4,128)} %copy.202), channel_id=1, source_target_pairs={{4,0},{8,4},{12,8},{16,12},{20,16},{24,20},{28,24},{0,28},{5,1},{9... | collective-permute-start | bytes 7864328 | tf_op jit(solution)/shard_map/ppermute | solution.py:12
  11.7 132.5 %collective-permute-start.1 = (f32[4,2,5,16384]{3,0,2,1:T(4,128)}, f32[4,2,5,16384]{3,0,2,1:T(4,128)}, u32[]{:S(2)}, u32[]{:S(2)}) collective-permute-start(f32[4,2,5,16384]{3,0,2,1:T(4,128)} %copy.202), channel_id=1, source_target_pairs={{28,0},{0,4},{4,8},{8,12},{12,16},{16,20},{20,24},{24,28},{29,1},{... | collective-permute-start | bytes 7864328 | tf_op jit(solution)/shard_map/ppermute | solution.py:12
  28.3 5.4 %copy-start.16 = (s32[4]{0:T(128)S(1)}, s32[4]{0:T(128)}, u32[]{:S(2)}) copy-start(s32[4]{0:T(128)} %param.20) | copy-start | bytes 52
  28.3 5.4 %copy-start.9 = (f32[4,5,2,4]{1,3,2,0:T(4,128)S(1)}, f32[4,5,2,4]{1,3,2,0:T(4,128)}, u32[]{:S(2)}) copy-start(f32[4,5,2,4]{1,3,2,0:T(4,128)} %param.19) | copy-start | bytes 1924
  28.3 5.6 %copy-start.11 = (f32[16384]{0:T(1024)S(1)}, f32[16384]{0:T(1024)}, u32[]{:S(2)}) copy-start(f32[16384]{0:T(1024)} %param.18) | copy-start | bytes 196612
  28.3 32.2 %collective-permute-start = (f32[4,2,5,1024]{3,1,2,0:T(2,128)S(1)}, f32[4,2,5,1024]{3,1,2,0:T(2,128)}, u32[]{:S(2)}, u32[]{:S(2)}) collective-permute-start(f32[4,2,5,1024]{3,1,2,0:T(2,128)S(1)} %broadcast_select_fusion), channel_id=1, source_target_pairs={{0,1},{1,2},{2,3},{4,5},{5,6},{6,7},{8,9},{9,10},{10,11},{12,13},{... | collective-permute-start | bytes 491528 | tf_op jit(solution)/shard_map/ppermute | solution.py:18
  52.8 2.8 copy-start.10
  52.8 3.1 copy-start.12
  52.8 3.1 copy-start.13
  52.9 3.2 copy-start.14
  89.0 2.6 copy-start.5
  136.3 114.7 %collective-permute-start.4 = (f32[4,2,5,16384]{3,0,2,1:T(4,128)}, f32[4,2,5,16384]{3,0,2,1:T(4,128)S(1)}, u32[]{:S(2)}, u32[]{:S(2)}) collective-permute-start(f32[4,2,5,16384]{3,0,2,1:T(4,128)} %collective-permute-done.2), channel_id=1, source_target_pairs={{4,0},{8,4},{12,8},{16,12},{20,16},{24,20},{28,24},{0,28},{5,1},{9... | collective-permute-start | bytes 7864328 | tf_op jit(solution)/shard_map/ppermute | solution.py:12
  158.9 106.5 %collective-permute-start.3 = (f32[4,2,5,16384]{3,0,2,1:T(4,128)}, f32[4,2,5,16384]{3,0,2,1:T(4,128)S(1)}, u32[]{:S(2)}, u32[]{:S(2)}) collective-permute-start(f32[4,2,5,16384]{3,0,2,1:T(4,128)} %collective-permute-done.1), channel_id=1, source_target_pairs={{28,0},{0,4},{4,8},{8,12},{12,16},{16,20},{20,24},{24,28},{29,1},{... | collective-permute-start | bytes 7864328 | tf_op jit(solution)/shard_map/ppermute | solution.py:12
  272.3 7.4 %copy-start.8 = (f32[4,1,5,16384]{3,2,1,0:T(8,128)S(1)}, f32[4,1,5,16384]{3,2,1,0:T(8,128)}, u32[]{:S(2)}) copy-start(f32[4,1,5,16384]{3,2,1,0:T(8,128)} %get-tuple-element.31) | copy-start | bytes 3932164
  274.7 5.0 %copy-start.4 = (f32[4,2,5,16384]{3,2,1,0:T(8,128)S(1)}, f32[4,2,5,16384]{3,2,1,0:T(8,128)}, u32[]{:S(2)}) copy-start(f32[4,2,5,16384]{3,2,1,0:T(8,128)} %reshape.205) | copy-start | bytes 7864324
  274.7 5.0 %copy-start.6 = (f32[4,1,5,16384]{3,2,1,0:T(8,128)S(1)}, f32[4,1,5,16384]{3,2,1,0:T(8,128)}, u32[]{:S(2)}) copy-start(f32[4,1,5,16384]{3,2,1,0:T(8,128)} %fusion.18) | copy-start | bytes 3932164
  274.7 5.0 %copy-start.7 = (f32[4,1,5,16384]{3,2,1,0:T(8,128)S(1)}, f32[4,1,5,16384]{3,2,1,0:T(8,128)}, u32[]{:S(2)}) copy-start(f32[4,1,5,16384]{3,2,1,0:T(8,128)} %fusion.17) | copy-start | bytes 3932164
  290.8 4.3 %copy-start.1 = (f32[4,2,5,16384]{3,2,1,0:T(8,128)}, f32[4,2,5,16384]{3,2,1,0:T(8,128)S(1)}, u32[]{:S(2)}) copy-start(f32[4,2,5,16384]{3,2,1,0:T(8,128)S(1)} %fusion.2) | copy-start | bytes 7864324
  290.8 4.3 %copy-start.17 = (s32[4]{0:T(128)S(1)}, s32[4]{0:T(128)}, u32[]{:S(2)}) copy-start(s32[4]{0:T(128)} %param.21) | copy-start | bytes 52
  292.5 114.3 %collective-permute-start.5 = (f32[4,2,5,16384]{3,0,2,1:T(4,128)S(1)}, f32[4,2,5,16384]{3,0,2,1:T(4,128)S(1)}, u32[]{:S(2)}, u32[]{:S(2)}) collective-permute-start(f32[4,2,5,16384]{3,0,2,1:T(4,128)S(1)} %copy.220), channel_id=1, source_target_pairs={{0,16},{16,0},{4,20},{20,4},{8,24},{24,8},{12,28},{28,12},{1,17},{... | collective-permute-start | bytes 7864328 | tf_op jit(solution)/shard_map/ppermute | solution.py:28
  417.2 2.2 copy-start.2
where the time goes:
time: 430 us; the launch traced here: 424 us
  waiting for transfers between devices  217 us (50%)
  matrix products  75.9 us (18%)
  local copies, waits for them, and re-layouts  72.5 us (17%)
  other arithmetic  43.2 us (10%)
  starting transfers between devices  14.1 us (3%)
    ppermute x4, waiting for transfers between devices, shifted(): return lax.ppermute(block, axis, route)  108 us
    ppermute x1, waiting for transfers between devices, from_partner(): return lax.ppermute(block, axis, route)  108 us
    another operation x6, other arithmetic, couple_tap(): jnp.stack([real_part, imag_part], axis=1)  25.6 us
    dot_general x5, matrix products, couple_tap(): jnp.einsum('ab,bvx->avx', imag_w, panel[:, 1], precision=highest)  15.3 us
    dot_general x5, matrix products, couple_tap(): jnp.einsum('ab,bvx->avx', real_w, panel[:, 1], precision=highest)  15.1 us
    dot_general x5, matrix products, couple_tap(): jnp.einsum('ab,bvx->avx', imag_w, panel[:, 0], precision=highest)  14.6 us
    dot_general x5, matrix products, couple_tap(): jnp.einsum('ab,bvx->avx', real_w, panel[:, 0], precision=highest)  14.6 us
    unnamed x39, local copies, waits for them, and re-layouts  14 us
  transfers between devices with their start and end apart: 6, of which 3 were waited for; matrix products, arithmetic and copies ran while one was open for 34% of the time, Pallas kernels for 0%

commit v1 on v0

v1 whole, which is shorter than its diff:
```python
import jax
import jax.numpy as jnp
from jax import lax
from jax.experimental import pallas as pl
from jax.experimental.pallas import tpu as pltpu
from jax.sharding import PartitionSpec as P

TAPS = 5
BLOCK = 32
LANES = 128
MESH = pl.DeviceIdType.MESH


def split(x):
    high = x.astype(jnp.bfloat16)
    low = (x - high.astype(jnp.float32)).astype(jnp.bfloat16)
    return high, low


def dot(a, b):
    return jnp.dot(a, b, preferred_element_type=jnp.float32)


def times_i(x):
    even = lax.broadcasted_iota(jnp.int32, x.shape, 0) % 2 == 0
    return jnp.where(even, -pltpu.roll(x, x.shape[0] - 1, 0), pltpu.roll(x, 1, 0))


def doubled(x, half):
    low = lax.broadcasted_iota(jnp.int32, x.shape, 1) < LANES // 2
    other = pltpu.roll(x, LANES // 2, 1)
    return jnp.where(low, x, other) if half == 0 else jnp.where(low, other, x)


def by_half(x, y):
    return jnp.where(lax.broadcasted_iota(jnp.int32, x.shape, 1) < LANES // 2, x, y)


def kernel(
    coup,
    jac,
    fac,
    perm,
    adj,
    src,
    kmat,
    pick,
    pick_halo,
    harm,
    swirl,
    res,
    sens,
    near,
    opp,
    mer,
    faces,
    halo,
    send_sem,
    recv_sem,
    halo_sem,
):
    modes, nv, rows, _ = adj.shape
    frows = faces.shape[2]
    n_mode = lax.axis_size("mode")
    n_slab = lax.axis_size("slab")
    me = lax.axis_index("mode")
    slab = lax.axis_index("slab")
    odd = me % 2
    above = (me + 2) % n_mode
    below = (me + n_mode - 2) % n_mode
    pair = me + 1 - 2 * odd
    across = (me + n_mode // 2) % n_mode
    after = (slab + 1) % n_slab
    before = (slab + n_slab - 1) % n_slab

    barrier = pltpu.get_barrier_semaphore()
    for other in (above, below, pair, across):
        pl.semaphore_signal(barrier, inc=1, device_id=(other, slab), device_id_type=MESH)
    for other in (after, before):
        pl.semaphore_signal(barrier, inc=1, device_id=(me, other), device_id_type=MESH)
    pl.semaphore_wait(barrier, 6)

    def copy(kind, v, source, target, device):
        return pltpu.make_async_remote_copy(
            src_ref=source.at[:, v],
            dst_ref=target.at[:, v],
            send_sem=send_sem.at[kind, v],
            recv_sem=recv_sem.at[kind, v],
            device_id=(device, slab),
            device_id_type=MESH,
        )

    def up(v):
        return copy(0, v, adj, near.at[0], above)

    def down(v):
        return copy(1, v, adj, near.at[1], below)

    def beside(v):
        return copy(2, v, adj, near.at[2], pair)

    def onward(v):
        return copy(3, v, near.at[1 - odd], near.at[3], pair)

    def over(v):
        return copy(4, v, res, opp, across)

    @pl.loop(0, nv)
    def _(v):
        up(v).start()
        down(v).start()
        beside(v).start()

    @pl.loop(0, modes * nv)
    def _(i):
        m = i // nv
        v = i % nv
        k_high, k_low = split(kmat[...])
        x_high, x_low = split(adj[m, v])
        lifted = dot(x_high, k_high) + dot(x_low, k_high) + dot(x_high, k_low)
        tall = jnp.concatenate([lifted[:, LANES : 2 * LANES], lifted[:, 2 * LANES :]], axis=0)
        picked = dot(pick[...], jnp.concatenate(split(tall), axis=1))
        picked = picked[:, :LANES] + picked[:, LANES:]
        mer[m, v] = lifted[:, :LANES] + by_half(picked[:rows], picked[rows : 2 * rows])
        faces[m, v] = by_half(
            picked[2 * rows : 2 * rows + frows], picked[2 * rows + frows :]
        )

    halo_copy = pltpu.make_async_remote_copy(
        src_ref=faces,
        dst_ref=halo,
        send_sem=halo_sem.at[0],
        recv_sem=halo_sem.at[1],
        device_id=(me, after),
        device_id_type=MESH,
    )
    halo_copy.start()

    def mix(total, values, tap, r0):
        turned = [times_i(x) for x in values]
        amplitude = harm[tap, pl.ds(r0, BLOCK), :]
        out = []
        for a in range(modes):
            at = (a * TAPS + tap) * 2 * modes
            part = values[0] * coup[at] + turned[0] * coup[at + modes]
            for b in range(1, modes):
                part = part + values[b] * coup[at + b] + turned[b] * coup[at + modes + b]
            out.append(total[a] - part * amplitude)
        return out

    @pl.loop(0, nv)
    def _(v):
        @pl.loop(0, rows // BLOCK)
        def _(j):
            r0 = pl.multiple_of(j * BLOCK, BLOCK)
            values = [adj[b, v, pl.ds(r0, BLOCK), :] for b in range(modes)]
            rate = swirl[pl.ds(r0, BLOCK), :]
            total = [
                src[a, v, pl.ds(r0, BLOCK), :] - times_i(values[a]) * (rate * fac[a])
                for a in range(modes)
            ]
            total = mix(total, values, TAPS // 2, r0)
            for a in range(modes):
                res[a, v, pl.ds(r0, BLOCK), :] = total[a]

    halo_copy.wait()
    present = jnp.where(slab == 0, 0.0, 1.0)

    @pl.loop(0, modes * nv)
    def _(i):
        m = i // nv
        v = i % nv
        got = halo[m, v] * present
        tall = jnp.concatenate([doubled(got, 0), doubled(got, 1)], axis=0)
        picked = dot(pick_halo[...], jnp.concatenate(split(tall), axis=1))
        picked = picked[:, :LANES] + picked[:, LANES:]
        mer[m, v] = mer[m, v] + by_half(picked[:rows], picked[rows:])

    @pl.loop(0, modes)
    def _(m):
        @pl.loop(0, rows // BLOCK)
        def _(j):
            r0 = pl.multiple_of(j * BLOCK, BLOCK)
            values = [mer[m, v, pl.ds(r0, BLOCK), :] for v in range(nv)]
            for w in range(nv):
                part = values[0] * jac[w * nv]
                for v in range(1, nv):
                    part = part + values[v] * jac[w * nv + v]
                res[m, w, pl.ds(r0, BLOCK), :] = res[m, w, pl.ds(r0, BLOCK), :] - part

    def add_mix(v, slots):
        @pl.loop(0, rows // BLOCK)
        def _(j):
            r0 = pl.multiple_of(j * BLOCK, BLOCK)
            total = [res[a, v, pl.ds(r0, BLOCK), :] for a in range(modes)]
            for slot, tap in slots:
                values = [near[slot, b, v, pl.ds(r0, BLOCK), :] for b in range(modes)]
                total = mix(total, values, tap, r0)
            for a in range(modes):
                res[a, v, pl.ds(r0, BLOCK), :] = total[a]

    @pl.loop(0, nv)
    def _(v):
        up(v).wait_recv()
        down(v).wait_recv()
        onward(v).start()
        beside(v).wait_recv()
        add_mix(v, ((0, 4), (1, 0), (2, 1 + 2 * odd)))
        onward(v).wait_recv()
        add_mix(v, ((3, 3 - 2 * odd),))
        over(v).start()

    @pl.loop(0, nv)
    def _(v):
        over(v).wait_recv()

        @pl.loop(0, rows // BLOCK)
        def _(j):
            r0 = pl.multiple_of(j * BLOCK, BLOCK)
            even = lax.broadcasted_iota(jnp.int32, (BLOCK, LANES), 0) % 2 == 0
            values = [opp[b, v, pl.ds(r0, BLOCK), :] for b in range(modes)]
            values = [jnp.where(even, x, -x) for x in values]
            for a in range(modes):
                total = res[a, v, pl.ds(r0, BLOCK), :]
                for b in range(modes):
                    total = total + values[b] * perm[a * modes + b]
                sens[a, v, pl.ds(r0, BLOCK), :] = total

    @pl.loop(0, nv)
    def _(v):
        up(v).wait_send()
        down(v).wait_send()
        beside(v).wait_send()
        onward(v).wait_send()
        over(v).wait_send()


def per_device(
    adjoint,
    source,
    derivative,
    lift_matrix,
    jacobian,
    harmonics,
    swirl_rate,
    coupling,
    mode_number,
    partner,
    upstream,
    face_list,
):
    modes, _, nv, cells = adjoint.shape
    nodes = derivative.shape[0]
    elements = cells // nodes
    face_count = face_list.shape[0]
    tiles = cells // LANES
    rows = 2 * tiles
    frows = face_count
    highest_mode = modes * lax.axis_size("mode") // 2

    def to_rows(x):
        x = x.reshape(modes, 2, nv, tiles, LANES)
        return x.transpose(0, 2, 3, 1, 4).reshape(modes, nv, rows, LANES)

    def from_rows(x):
        x = x.reshape(modes, nv, tiles, 2, LANES)
        return x.transpose(0, 3, 1, 2, 4).reshape(modes, 2, nv, cells)

    eye = jnp.eye(2, dtype=jnp.float32)
    lift = lift_matrix.T
    nothing = jnp.zeros_like(lift)
    kmat = jnp.concatenate(
        [
            jnp.kron(eye, derivative.T),
            jnp.block([[lift, lift], [nothing, nothing]]),
            jnp.block([[nothing, nothing], [lift, lift]]),
        ],
        axis=1,
    )

    def spread(values):
        values = values.reshape(-1, 2).T
        return jnp.repeat(values.reshape(-1), 2)

    def match(wanted, held):
        part = jnp.arange(wanted.shape[0]) % 2
        part_held = jnp.arange(held.shape[0]) % 2
        same = (wanted[:, None] == held[None, :]) & (part[:, None] == part_held[None, :])
        return same.astype(jnp.bfloat16)

    element = spread(jnp.arange(elements, dtype=jnp.int32))
    face = spread(jnp.arange(face_count, dtype=jnp.int32))
    wanted = spread(upstream)
    pick = match(
        jnp.concatenate([wanted - face_count, spread(face_list)]), element
    )
    pick_halo = match(wanted, face)
    harm = jnp.repeat(harmonics.reshape(TAPS, tiles, LANES), 2, axis=1)
    swirl = jnp.repeat(swirl_rate.reshape(tiles, LANES), 2, axis=0)
    factor = mode_number.astype(jnp.float32) / highest_mode
    perm = (partner[:, None] % modes == jnp.arange(modes)[None, :]).astype(jnp.float32)

    panel = (modes, nv, rows, LANES)
    small = (modes, nv, frows, LANES)
    smem = pl.BlockSpec(memory_space=pltpu.SMEM)
    vmem = pl.BlockSpec(memory_space=pltpu.VMEM)
    residual, sensitivity = pl.pallas_call(
        kernel,
        out_shape=[jax.ShapeDtypeStruct(panel, jnp.float32)] * 2,
        in_specs=[smem] * 4 + [vmem] * 7,
        out_specs=[vmem] * 2,
        scratch_shapes=[
            pltpu.VMEM((4,) + panel, jnp.float32),
            pltpu.VMEM(panel, jnp.float32),
            pltpu.VMEM(panel, jnp.float32),
            pltpu.VMEM(small, jnp.float32),
            pltpu.VMEM(small, jnp.float32),
            pltpu.SemaphoreType.DMA((5, nv)),
            pltpu.SemaphoreType.DMA((5, nv)),
            pltpu.SemaphoreType.DMA((2,)),
        ],
        compiler_params=pltpu.CompilerParams(
            collective_id=0, has_side_effects=True, vmem_limit_bytes=48 * 1024 * 1024
        ),
    )(
        coupling.reshape(-1),
        jacobian.reshape(-1),
        factor,
        perm.reshape(-1),
        to_rows(adjoint),
        to_rows(source),
        kmat,
        pick,
        pick_halo,
        harm,
        swirl,
    )
    return (from_rows(residual), from_rows(sensitivity))


def solution(mesh):
    in_specs = (
        P("mode", None, None, "slab"),
        P("mode", None, None, "slab"),
        P(),
        P(),
        P(),
        P(None, "slab"),
        P("slab"),
        P("mode", None, None, None),
        P("mode"),
        P("mode"),
        P("slab"),
        P("slab"),
    )
    out_specs = (P("mode", None, None, "slab"), P("mode", None, None, "slab"))
    return jax.shard_map(
        per_device, mesh=mesh, in_specs=in_specs, out_specs=out_specs, check_vma=False
    )
```

time: 430 us -> 252 us (0.59); the launches traced: 424 us -> 252 us
  Pallas kernels: 0 us -> 236 us
  waiting for transfers between devices: 217 us -> 0 us
  matrix products: 75.9 us -> 0 us
  local copies, waits for them, and re-layouts: 72.5 us -> 12.7 us
  other arithmetic: 43.2 us -> 2.07 us
  starting transfers between devices: 14.1 us -> 0 us
    pallas_call x0 -> x1, Pallas kernels: none -> 236 us  [per_device(): pl.pallas_call(kernel, out_shape=[jax.ShapeDtypeStruct(panel, jnp.float32...]
    ppermute x6 -> x0, waiting for transfers between devices: 217 us -> none  [the longest x4 108 us: shifted(): return lax.ppermute(block, axis, route)]
    dot_general x23 -> x0, matrix products: 75.9 us -> none  [the longest x5 15.3 us: couple_tap(): jnp.einsum('ab,bvx->avx', imag_w, panel[:, 1], precision=highest)]
    another operation x6 -> x0, other arithmetic: 25.6 us -> none  [couple_tap(): jnp.stack([real_part, imag_part], axis=1)]
    gather x5 -> x0, local copies, waits for them, and re-layouts: 17.8 us -> none  [the longest x1 9.22 us: per_device(): upper = jnp.take(extended, upstream, axis=3)]
    reshape x6 -> x8, local copies, waits for them, and re-layouts: 20.4 us -> 2.83 us  [the longest x3 1.63 us: spread(): values = values.reshape(-1, 2).T]
    ppermute x6 -> x0, starting transfers between devices: 14.1 us -> none  [the longest x4 9.1 us: shifted(): return lax.ppermute(block, axis, route)]
    select_n x2 -> x0, local copies, waits for them, and re-layouts: 7.21 us -> none  [per_device(): upper = jnp.take(extended, upstream, axis=3)]
  transfers between devices with their start and end apart: 6 -> 0, of which waited for: 3 -> 0; matrix products, arithmetic and copies ran while one was open for 34% -> 0% of each run, Pallas kernels for 0% -> 0%
where the time goes in v1:
time: 252 us
  Pallas kernels  236 us (94%)
  local copies, waits for them, and re-layouts  12.7 us (5%)
    pallas_call x1, Pallas kernels, per_device(): pl.pallas_call(kernel, out_shape=[jax.ShapeDtypeStruct(panel, jnp.float32...  236 us
    unnamed x7, local copies, waits for them, and re-layouts  6.97 us

profile of v1, /device:TPU:0, one launch (start us, length us, event | category | flops | bytes accessed | tf_op | source)
XLA Modules:
  0.0 251.6 jit_solution(16589993538265527594)
XLA Ops:
  0.6 0.8 reshape.162.jac
  1.4 0.7 convert_multiply_fusion.fac
  2.1 0.7 and_select_fusion.1
  3.0 0.7 reshape.170
  4.0 0.1 reshape.172
  4.1 0.1 eq.99
  4.2 0.8 copy.30
  5.1 0.1 reshape.161.coup
  5.2 0.8 copy.33
  6.0 0.8 copy.34
  6.9 0.8 reshape.167
  7.8 0.1 broadcast_multiply_fusion
  7.9 0.1 mul.27
  8.2 0.1 reshape.169
  8.4 0.2 and_convert_fusion.1.pick_halo
  8.7 0.1 eq.92
  8.9 0.9 broadcast_in_dim.38
  9.8 1.1 copy.43
  10.9 0.2 broadcast_in_dim.37
  11.1 0.2 and_convert_fusion.pick
  11.3 236.1 %shard_map.131 = (f32[4,5,256,128]{3,2,1,0:T(8,128)S(1)}, f32[4,5,256,128]{3,2,1,0:T(8,128)}) custom-call(f32[160]{0:T(256)S(1)} %reshape.161.coup, f32[25]{0:T(128)S(1)} %reshape.162.jac, f32[4]{0:T(128)S(1)} %convert_multiply_fusion.fac, f32[16]{0:T(128)S(1)} %reshape.189.perm, f32[4,5,256,128]{3,2,1,0:T(8,128)} %bitcast.37, f32[4,5,256,128]{3,2,1,0:T(8,128)} %bitcast.38, ...), custom_call_target="tpu_custom_call" | custom-call | tf_op jit(solution)/shard_map/pallas_call | solution.py:307
  247.4 1.5 copy.46
  248.9 1.2 copy-done
  250.1 1.5 copy.47
  (22 shorter events, 0.9 us)
Async XLA Ops:
  247.4 2.7 %copy-start = (f32[4,5,256,128]{3,2,1,0:T(8,128)S(1)}, f32[4,5,256,128]{3,2,1,0:T(8,128)}, u32[]{:S(2)}) copy-start(f32[4,5,256,128]{3,2,1,0:T(8,128)} %get-tuple-element.5) | copy-start | bytes 7864324

commit v2 on v1

v2 whole, which is shorter than its diff:
```python
import jax
import jax.numpy as jnp
from jax import lax
from jax.experimental import pallas as pl
from jax.experimental.pallas import tpu as pltpu
from jax.sharding import PartitionSpec as P

TAPS = 5
BLOCK = 32
LANES = 128
WINDOW = 3
MESH = pl.DeviceIdType.MESH


def split(x):
    high = x.astype(jnp.bfloat16)
    low = (x - high.astype(jnp.float32)).astype(jnp.bfloat16)
    return high, low


def dot(a, b):
    return jnp.dot(a, b, preferred_element_type=jnp.float32)


def dot_t(a, b):
    return lax.dot_general(a, b, (((1,), (1,)), ((), ())), preferred_element_type=jnp.float32)


def times_i(x):
    even = lax.broadcasted_iota(jnp.int32, x.shape, 0) % 2 == 0
    return jnp.where(even, -pltpu.roll(x, x.shape[0] - 1, 0), pltpu.roll(x, 1, 0))


def doubled(x, half):
    low = lax.broadcasted_iota(jnp.int32, x.shape, 1) < LANES // 2
    other = pltpu.roll(x, LANES // 2, 1)
    return jnp.where(low, x, other) if half == 0 else jnp.where(low, other, x)


def by_half(x, y):
    return jnp.where(lax.broadcasted_iota(jnp.int32, x.shape, 1) < LANES // 2, x, y)


def spot(i, span):
    return (i % span) // 2 * 2 + i // span


def kernel(
    coup,
    jac,
    number,
    partner,
    adj_hbm,
    src_hbm,
    derivative,
    lift,
    upstream,
    face_list,
    harm_in,
    swirl_in,
    res,
    sens,
    adj,
    src,
    near,
    opp,
    mer,
    faces,
    halo,
    kmat,
    pick,
    pick_halo,
    harm,
    swirl,
    send_sem,
    recv_sem,
    halo_sem,
    load_sem,
):
    modes, nv, rows, _ = adj.shape
    chunks = 2 * nv
    part = rows // 2
    frows = faces.shape[2]
    n_mode = lax.axis_size("mode")
    n_slab = lax.axis_size("slab")
    me = lax.axis_index("mode")
    slab = lax.axis_index("slab")
    odd = me % 2
    above = (me + 2) % n_mode
    below = (me + n_mode - 2) % n_mode
    pair = me + 1 - 2 * odd
    across = (me + n_mode // 2) % n_mode
    after = (slab + 1) % n_slab
    before = (slab + n_slab - 1) % n_slab

    load_adj = pltpu.make_async_copy(adj_hbm, adj, load_sem.at[0])
    load_src = pltpu.make_async_copy(src_hbm, src, load_sem.at[1])
    load_adj.start()
    load_src.start()

    barrier = pltpu.get_barrier_semaphore()
    for other in (above, below, pair, across):
        pl.semaphore_signal(barrier, inc=1, device_id=(other, slab), device_id_type=MESH)
    for other in (after, before):
        pl.semaphore_signal(barrier, inc=1, device_id=(me, other), device_id_type=MESH)
    pl.semaphore_wait(barrier, 6)
    load_adj.wait()

    def place(q):
        return q // 2, pl.multiple_of(q % 2 * part, part)

    def copy(kind, q, source, target, device):
        v, r0 = place(q)
        return pltpu.make_async_remote_copy(
            src_ref=source.at[:, v, pl.ds(r0, part)],
            dst_ref=target.at[:, v, pl.ds(r0, part)],
            send_sem=send_sem.at[kind, q],
            recv_sem=recv_sem.at[kind, q],
            device_id=(device, slab),
            device_id_type=MESH,
        )

    def up(q):
        return copy(0, q, adj, near.at[0], above)

    def down(q):
        return copy(1, q, adj, near.at[1], below)

    def beside(q):
        return copy(2, q, adj, near.at[2], pair)

    def onward(q):
        return copy(3, q, near.at[1 - odd], near.at[3], pair)

    def over(q):
        return copy(4, q, res, opp, across)

    def begin(q):
        up(q).start()
        down(q).start()
        beside(q).start()

    @pl.loop(0, WINDOW)
    def _(q):
        begin(q)

    def arrive(q):
        up(q).wait_send()
        down(q).wait_send()

        @pl.when(q + WINDOW < chunks)
        def _():
            begin(q + WINDOW)

        up(q).wait_recv()
        down(q).wait_recv()
        onward(q).start()
        beside(q).wait_recv()

    span = rows
    d = derivative[...]
    low = lift[...]
    none = jnp.zeros_like(d)
    kmat[...] = jnp.concatenate(
        [
            jnp.concatenate([d, none], axis=1),
            jnp.concatenate([none, d], axis=1),
            jnp.concatenate([low, none], axis=1),
            jnp.concatenate([low, none], axis=1),
            jnp.concatenate([none, low], axis=1),
            jnp.concatenate([none, low], axis=1),
        ],
        axis=0,
    )

    def iota(shape, axis):
        return lax.broadcasted_iota(jnp.int32, shape, axis)

    def wanted_rows(values, count, span_out):
        held = values.shape[1]
        mine = spot(iota((count, held), 0), span_out)
        chosen = jnp.where(mine == iota((count, held), 1), values, 0.0)
        return jnp.sum(chosen, axis=1, keepdims=True)

    def one_hot(wanted, count, width, span_in):
        held = spot(iota((count, width), 1), span_in).astype(jnp.float32)
        same = (iota((count, width), 0) % 2) == (iota((count, width), 1) % 2)
        hot = jnp.where(wanted == held, 1.0, 0.0)
        return jnp.where(same, hot, 0.0).astype(jnp.bfloat16)

    source_row = wanted_rows(upstream[...].astype(jnp.float32), 2 * rows, span)
    face_row = wanted_rows(face_list[...].astype(jnp.float32), 2 * frows, frows)
    pick[: 2 * rows] = one_hot(source_row - float(frows), 2 * rows, 2 * rows, span)
    pick[2 * rows :] = one_hot(face_row, 2 * frows, 2 * rows, span)
    pick_halo[...] = one_hot(source_row, 2 * rows, 2 * frows, frows)

    twice = jnp.where(
        iota((rows, rows // 2), 0) // 2 == iota((rows, rows // 2), 1), 1.0, 0.0
    ).astype(jnp.bfloat16)

    def double(x):
        high = x.astype(jnp.bfloat16)
        rest, last = split(x - high.astype(jnp.float32))
        return dot(twice, high) + dot(twice, rest) + dot(twice, last)

    for tap in range(TAPS):
        harm[tap] = double(harm_in[:, tap, :])
    swirl[...] = double(swirl_in[...])
    load_src.wait()

    half_modes = float(modes * n_mode // 2)
    fac = [number[a].astype(jnp.float32) / half_modes for a in range(modes)]

    def gather(i):
        m = i // nv
        v = i % nv
        k_high, k_low = split(kmat[...])
        x_high, x_low = split(adj[m, v])
        lifted = dot_t(x_high, k_high) + dot_t(x_low, k_high) + dot_t(x_high, k_low)
        tall = jnp.concatenate([lifted[:, LANES : 2 * LANES], lifted[:, 2 * LANES :]], axis=0)
        picked = dot(pick[...], jnp.concatenate(split(tall), axis=1))
        picked = picked[:, :LANES] + picked[:, LANES:]
        mer[m, v] = lifted[:, :LANES] + by_half(picked[:rows], picked[rows : 2 * rows])
        faces[m, v] = by_half(
            picked[2 * rows : 2 * rows + frows], picked[2 * rows + frows :]
        )

    halo_copy = pltpu.make_async_remote_copy(
        src_ref=faces,
        dst_ref=halo,
        send_sem=halo_sem.at[0],
        recv_sem=halo_sem.at[1],
        device_id=(me, after),
        device_id_type=MESH,
    )

    def mix(total, values, tap, r0):
        turned = [times_i(x) for x in values]
        amplitude = harm[tap, pl.ds(r0, BLOCK), :]
        out = []
        for a in range(modes):
            at = a * 2 * modes
            term = values[0] * coup[at, tap] + turned[0] * coup[at + modes, tap]
            for b in range(1, modes):
                term = term + values[b] * coup[at + b, tap]
                term = term + turned[b] * coup[at + modes + b, tap]
            out.append(total[a] - term * amplitude)
        return out

    def direct(q):
        v, start = place(q)

        @pl.loop(0, part // BLOCK)
        def _(j):
            r0 = pl.multiple_of(start + j * BLOCK, BLOCK)
            values = [adj[b, v, pl.ds(r0, BLOCK), :] for b in range(modes)]
            rate = swirl[pl.ds(r0, BLOCK), :]
            total = [
                src[a, v, pl.ds(r0, BLOCK), :] - times_i(values[a]) * (rate * fac[a])
                for a in range(modes)
            ]
            total = mix(total, values, TAPS // 2, r0)
            for slot, tap in ((0, 4), (1, 0), (2, 1 + 2 * odd)):
                values = [near[slot, b, v, pl.ds(r0, BLOCK), :] for b in range(modes)]
                total = mix(total, values, tap, r0)
            for a in range(modes):
                res[a, v, pl.ds(r0, BLOCK), :] = total[a]

    def finish(q):
        onward(q).wait_recv()
        v, start = place(q)

        @pl.loop(0, part // BLOCK)
        def _(j):
            r0 = pl.multiple_of(start + j * BLOCK, BLOCK)
            total = []
            for a in range(modes):
                term = res[a, v, pl.ds(r0, BLOCK), :]
                for w in range(nv):
                    term = term - mer[a, w, pl.ds(r0, BLOCK), :] * jac[v, w]
                total.append(term)
            values = [near[3, b, v, pl.ds(r0, BLOCK), :] for b in range(modes)]
            total = mix(total, values, 3 - 2 * odd, r0)
            for a in range(modes):
                res[a, v, pl.ds(r0, BLOCK), :] = total[a]

    @pl.loop(0, nv)
    def _(q):
        @pl.loop(q * modes, (q + 1) * modes)
        def _(i):
            gather(i)

        arrive(q)
        direct(q)

    halo_copy.start()

    @pl.loop(nv, nv + 1)
    def _(q):
        arrive(q)
        direct(q)

    halo_copy.wait()
    present = jnp.where(slab == 0, 0.0, 1.0)

    @pl.loop(0, modes * nv)
    def _(i):
        m = i // nv
        v = i % nv
        got = halo[m, v] * present
        tall = jnp.concatenate([doubled(got, 0), doubled(got, 1)], axis=0)
        picked = dot(pick_halo[...], jnp.concatenate(split(tall), axis=1))
        picked = picked[:, :LANES] + picked[:, LANES:]
        mer[m, v] = mer[m, v] + by_half(picked[:rows], picked[rows:])

    @pl.loop(nv + 1, chunks)
    def _(q):
        @pl.when(q == chunks - 1)
        def _():
            over(0).start()

        arrive(q)
        direct(q)

        @pl.loop(2 * (q - nv - 1), 2 * (q - nv))
        def _(c):
            finish(c)

    @pl.loop(1, WINDOW)
    def _(q):
        over(q).start()

    @pl.loop(2 * (nv - 1), chunks)
    def _(q):
        finish(q)

    @pl.loop(0, chunks)
    def _(q):
        over(q).wait_send()

        @pl.when(q + WINDOW < chunks)
        def _():
            over(q + WINDOW).start()

        over(q).wait_recv()
        v, start = place(q)

        @pl.loop(0, part // BLOCK)
        def _(j):
            r0 = pl.multiple_of(start + j * BLOCK, BLOCK)
            even = iota((BLOCK, LANES), 0) % 2 == 0
            values = [opp[b, v, pl.ds(r0, BLOCK), :] for b in range(modes)]
            values = [jnp.where(even, x, -x) for x in values]
            for a in range(modes):
                total = res[a, v, pl.ds(r0, BLOCK), :]
                mate = partner[a] % modes
                for b in range(modes):
                    total = total + values[b] * jnp.where(mate == b, 1.0, 0.0)
                sens[a, v, pl.ds(r0, BLOCK), :] = total

    @pl.loop(0, chunks)
    def _(q):
        beside(q).wait_send()
        onward(q).wait_send()


def per_device(
    adjoint,
    source,
    derivative,
    lift_matrix,
    jacobian,
    harmonics,
    swirl_rate,
    coupling,
    mode_number,
    partner,
    upstream,
    face_list,
):
    modes, _, nv, cells = adjoint.shape
    face_count = face_list.shape[0]
    tiles = cells // LANES
    rows = 2 * tiles
    frows = face_count

    def to_rows(x):
        x = x.reshape(modes, 2, nv, tiles, LANES)
        return x.transpose(0, 2, 3, 1, 4).reshape(modes, nv, rows, LANES)

    def from_rows(x):
        x = x.reshape(modes, nv, tiles, 2, LANES)
        return x.transpose(0, 3, 1, 2, 4).reshape(modes, 2, nv, cells)

    panel = (modes, nv, rows, LANES)
    small = (modes, nv, frows, LANES)
    smem = pl.BlockSpec(memory_space=pltpu.SMEM)
    vmem = pl.BlockSpec(memory_space=pltpu.VMEM)
    hbm = pl.BlockSpec(memory_space=pl.ANY)
    residual, sensitivity = pl.pallas_call(
        kernel,
        out_shape=[jax.ShapeDtypeStruct(panel, jnp.float32)] * 2,
        in_specs=[smem] * 4 + [hbm] * 2 + [vmem] * 6,
        out_specs=[vmem] * 2,
        scratch_shapes=[
            pltpu.VMEM(panel, jnp.float32),
            pltpu.VMEM(panel, jnp.float32),
            pltpu.VMEM((4,) + panel, jnp.float32),
            pltpu.VMEM(panel, jnp.float32),
            pltpu.VMEM(panel, jnp.float32),
            pltpu.VMEM(small, jnp.float32),
            pltpu.VMEM(small, jnp.float32),
            pltpu.VMEM((3 * LANES, LANES), jnp.float32),
            pltpu.VMEM((2 * rows + 2 * frows, 2 * rows), jnp.bfloat16),
            pltpu.VMEM((2 * rows, 2 * frows), jnp.bfloat16),
            pltpu.VMEM((TAPS, rows, LANES), jnp.float32),
            pltpu.VMEM((rows, LANES), jnp.float32),
            pltpu.SemaphoreType.DMA((5, 2 * nv)),
            pltpu.SemaphoreType.DMA((5, 2 * nv)),
            pltpu.SemaphoreType.DMA((2,)),
            pltpu.SemaphoreType.DMA((2,)),
        ],
        compiler_params=pltpu.CompilerParams(
            collective_id=0, has_side_effects=True, vmem_limit_bytes=60 * 1024 * 1024
        ),
    )(
        coupling.transpose(0, 2, 3, 1).reshape(modes * 2 * modes, TAPS),
        jacobian,
        mode_number,
        partner,
        to_rows(adjoint),
        to_rows(source),
        derivative,
        lift_matrix,
        upstream.reshape(1, -1),
        face_list.reshape(1, -1),
        harmonics.reshape(TAPS, tiles, LANES).transpose(1, 0, 2),
        swirl_rate.reshape(tiles, LANES),
    )
    return (from_rows(residual), from_rows(sensitivity))


def solution(mesh):
    in_specs = (
        P("mode", None, None, "slab"),
        P("mode", None, None, "slab"),
        P(),
        P(),
        P(),
        P(None, "slab"),
        P("slab"),
        P("mode", None, None, None),
        P("mode"),
        P("mode"),
        P("slab"),
        P("slab"),
    )
    out_specs = (P("mode", None, None, "slab"), P("mode", None, None, "slab"))
    return jax.shard_map(
        per_device, mesh=mesh, in_specs=in_specs, out_specs=out_specs, check_vma=False
    )
```

time: 252 us -> 242 us (0.960)
  local copies, waits for them, and re-layouts: 12.7 us -> 5.13 us
    reshape x8 -> x0, local copies, waits for them, and re-layouts: 2.83 us -> none  [the longest x3 1.63 us: spread(): values = values.reshape(-1, 2).T]
    unnamed x7 -> x4, local copies, waits for them, and re-layouts: 6.97 us -> 5.13 us
where the time goes in v2:
time: 242 us
  Pallas kernels  236 us (98%)
  local copies, waits for them, and re-layouts  5.13 us (2%)
    pallas_call x1, Pallas kernels, per_device(): pl.pallas_call(kernel, out_shape=[jax.ShapeDtypeStruct(panel, jnp.float32...  236 us
    unnamed x4, local copies, waits for them, and re-layouts  5.13 us

profile of v2, /device:TPU:0, one launch (start us, length us, event | category | flops | bytes accessed | tf_op | source)
XLA Modules:
  0.0 241.6 jit_solution(13752547145009002297)
XLA Ops:
  0.6 235.9 %shard_map.131 = (f32[4,5,256,128]{3,2,1,0:T(8,128)}, f32[4,5,256,128]{3,2,1,0:T(8,128)}) custom-call(f32[32,5]{1,0:T(8,128)} %bitcast.35, f32[5,5]{1,0:T(8,128)} %jac.1, s32[4]{0:T(128)} %number.1, s32[4]{0:T(128)} %partner.1, f32[4,5,256,128]{3,2,1,0:T(8,128)} %bitcast.29, f32[4,5,256,128]{3,2,1,0:T(8,128)} %bitcast.30, f32[64,64]{1,0:T(8,128)} %derivative.1, ...), custom_call_target="tpu_custom_call" | custom-call | tf_op jit(solution)/shard_map/pallas_call | solution.py:400
  236.5 0.0 copy-start
  236.5 3.6 %copy.20 = f32[4,2,5,16384]{3,1,2,0:T(2,128)} copy(f32[4,2,5,16384]{3,1,2,0:T(2,128)} %bitcast.32) | data formatting | bytes 5242880
  240.1 0.0 copy-done
  240.1 1.5 copy.21
Async XLA Ops:
  236.5 3.6 %copy-start = (f32[4,5,256,128]{3,2,1,0:T(8,128)S(1)}, f32[4,5,256,128]{3,2,1,0:T(8,128)}, u32[]{:S(2)}) copy-start(f32[4,5,256,128]{3,2,1,0:T(8,128)} %get-tuple-element.5) | copy-start | bytes 7864324

commit v3 on v2

--- a/solution.py
+++ b/solution.py
@@ -58,6 +58,8 @@
     face_list,
     harm_in,
     swirl_in,
+    res_hbm,
+    sens_hbm,
     res,
     sens,
     adj,
@@ -76,6 +78,7 @@
     recv_sem,
     halo_sem,
     load_sem,
+    save_sem,
 ):
     modes, nv, rows, _ = adj.shape
     chunks = 2 * nv
@@ -135,6 +138,14 @@
     def over(q):
         return copy(4, q, res, opp, across)
 
+    def save(kind, q):
+        v, r0 = place(q)
+        return pltpu.make_async_copy(
+            (res, sens)[kind].at[:, v, pl.ds(r0, part)],
+            (res_hbm, sens_hbm)[kind].at[:, v, pl.ds(r0, part)],
+            save_sem.at[kind, q],
+        )
+
     def begin(q):
         up(q).start()
         down(q).start()
@@ -284,6 +295,8 @@
             for a in range(modes):
                 res[a, v, pl.ds(r0, BLOCK), :] = total[a]
 
+        save(0, q).start()
+
     @pl.loop(0, nv)
     def _(q):
         @pl.loop(q * modes, (q + 1) * modes)
@@ -358,10 +371,14 @@
                     total = total + values[b] * jnp.where(mate == b, 1.0, 0.0)
                 sens[a, v, pl.ds(r0, BLOCK), :] = total
 
+        save(1, q).start()
+
     @pl.loop(0, chunks)
     def _(q):
         beside(q).wait_send()
         onward(q).wait_send()
+        save(0, q).wait()
+        save(1, q).wait()
 
 
 def per_device(
@@ -401,8 +418,10 @@
         kernel,
         out_shape=[jax.ShapeDtypeStruct(panel, jnp.float32)] * 2,
         in_specs=[smem] * 4 + [hbm] * 2 + [vmem] * 6,
-        out_specs=[vmem] * 2,
+        out_specs=[hbm] * 2,
         scratch_shapes=[
+            pltpu.VMEM(panel, jnp.float32),
+            pltpu.VMEM(panel, jnp.float32),
             pltpu.VMEM(panel, jnp.float32),
             pltpu.VMEM(panel, jnp.float32),
             pltpu.VMEM((4,) + panel, jnp.float32),
@@ -419,6 +438,7 @@
             pltpu.SemaphoreType.DMA((5, 2 * nv)),
             pltpu.SemaphoreType.DMA((2,)),
             pltpu.SemaphoreType.DMA((2,)),
+            pltpu.SemaphoreType.DMA((2, 2 * nv)),
         ],
         compiler_params=pltpu.CompilerParams(
             collective_id=0, has_side_effects=True, vmem_limit_bytes=60 * 1024 * 1024

time: 242 us -> 240 us (level)
  no operation moved by 1% of the time
where the time goes in v3:
time: 240 us
  Pallas kernels  234 us (98%)
  local copies, waits for them, and re-layouts  5.13 us (2%)
    pallas_call x1, Pallas kernels, per_device(): pl.pallas_call(kernel, out_shape=[jax.ShapeDtypeStruct(panel, jnp.float32...  234 us
    unnamed x4, local copies, waits for them, and re-layouts  5.13 us

profile of v3, /device:TPU:0, one launch (start us, length us, event | category | flops | bytes accessed | tf_op | source)
XLA Modules:
  0.0 240.1 jit_solution(14687129020536612610)
XLA Ops:
  0.6 234.3 %shard_map.131 = (f32[4,5,256,128]{3,2,1,0:T(8,128)}, f32[4,5,256,128]{3,2,1,0:T(8,128)}) custom-call(f32[32,5]{1,0:T(8,128)} %bitcast.35, f32[5,5]{1,0:T(8,128)} %jac.1, s32[4]{0:T(128)} %number.1, s32[4]{0:T(128)} %partner.1, f32[4,5,256,128]{3,2,1,0:T(8,128)} %bitcast.29, f32[4,5,256,128]{3,2,1,0:T(8,128)} %bitcast.30, f32[64,64]{1,0:T(8,128)} %derivative.1, ...), custom_call_target="tpu_custom_call" | custom-call | tf_op jit(solution)/shard_map/pallas_call | solution.py:417
  235.0 0.0 copy-start
  235.0 3.6 %copy.20 = f32[4,2,5,16384]{3,1,2,0:T(2,128)} copy(f32[4,2,5,16384]{3,1,2,0:T(2,128)} %bitcast.32) | data formatting | bytes 5242880
  238.6 0.0 copy-done
  238.6 1.5 copy.21
Async XLA Ops:
  235.0 3.6 %copy-start = (f32[4,5,256,128]{3,2,1,0:T(8,128)S(1)}, f32[4,5,256,128]{3,2,1,0:T(8,128)}, u32[]{:S(2)}) copy-start(f32[4,5,256,128]{3,2,1,0:T(8,128)} %get-tuple-element.5) | copy-start | bytes 7864324
